TPU v7x, 256 devices: a whole 4x4x8 slice. The times are simulated.
256 devices in a mesh: pair: 16 (over z_hi, y, core), ga: 16 (over z_lo, x).
Axes of the slice: x: 4, y: 4, z: 8 (z_hi: 2, z_lo: 4; z = z_hi * 4 + z_lo), core: 2. Of those that a mesh axis runs over, the one named last changes fastest.
Arguments:
- orbitals: bfloat16 [2, 8, 96, 18432], P(None, None, 'ga'), may hold values from -6 to 6
- owner: int32 [2, 8], replicated, may hold values from 0 to 7, each once within a row
- pair_list: int32 [64, 2], P('pair'), may hold values from 0 to 7
- valence_energy: float32 [8], replicated, may hold values from -12 to -2
- conduction_energy: float32 [8], replicated, may hold values from 0.5 to 6
- sphere_index: int32 [4096], replicated, may hold values from 0 to 1769471, as said below
Outputs:
- polarizability: float32 [2, 4096, 4096], P(None, 'ga', 'pair')
Inputs may be any that keep to these rules, and one draw needn't show every extreme that they name: `owner`: each row is a permutation of the 8 slots. `sphere_index`: 4096 distinct positions x * 96 * 192 + y * 192 + z whose signed frequencies f (index, less the grid length from the upper half on) give the smallest values of 4 fx^2 + 4 fy^2 + fz^2, in rising order of that value, equal values in a random order.
All inputs are finite; a program needn't handle non-finite values.
Results may differ from a plain program's by a relative error of at most 0.0003.
Values sent between devices are 32-bit elements; how exact they have to be, the bound alone decides.
A program may use at most 256 MiB of HBM per device.

v0:
```python
import math

import jax
import jax.numpy as jnp
from jax import lax
from jax.sharding import PartitionSpec as P

NX = 96
NY = 96
NZ = 192
NG = 4096


def twiddle_pair(length, points):
    position = jnp.arange(points, dtype=jnp.int32)
    frequency = jnp.arange(length, dtype=jnp.int32)
    turn_count = position[:, None] * frequency[None, :] % length
    phase_angle = turn_count.astype(jnp.float32) * (2.0 * math.pi / length)
    return (jnp.cos(phase_angle), jnp.sin(phase_angle))


def complex_table(length):
    cosine_table, sine_table = twiddle_pair(length, length)
    first = jnp.stack([cosine_table, -sine_table], -1)
    second = jnp.stack([sine_table, cosine_table], -1)
    return jnp.stack([first, second], 1)


def weighted_left(row_block, weights):
    scaled = row_block * weights[:, None, None]
    swapped = jnp.stack([scaled[:, 1], -scaled[:, 0]], 1)
    return jnp.stack([scaled, swapped], 0)


def per_device(orbitals, owner, pair_list, valence_energy, conduction_energy, sphere_index):
    highest = lax.Precision.HIGHEST
    band_count = orbitals.shape[1]
    planes = orbitals.shape[2]
    pairs_here = pair_list.shape[0]
    groups = lax.axis_size("ga")
    columns = NY // groups
    grid_index = lax.axis_index("ga")
    band_ids = jnp.arange(band_count, dtype=jnp.int32)
    pick_val = pair_list[:, 0][:, None] == band_ids[None, :]
    pick_con = pair_list[:, 1][:, None] == band_ids[None, :]
    slot_val = jnp.sum(jnp.where(pick_val, owner[0][None, :], 0), axis=1)
    slot_con = jnp.sum(jnp.where(pick_con, owner[1][None, :], 0), axis=1)
    energy_val = jnp.sum(jnp.where(pick_val, valence_energy[None, :], 0.0), axis=1)
    energy_con = jnp.sum(jnp.where(pick_con, conduction_energy[None, :], 0.0), axis=1)
    weights = 2.0 / (energy_val - energy_con)
    product = jnp.take(orbitals[0], slot_val, axis=0).astype(jnp.float32) * jnp.take(
        orbitals[1], slot_con, axis=0
    ).astype(jnp.float32)
    cosine_z, sine_z = twiddle_pair(NZ, NZ)
    table_z = jnp.concatenate([cosine_z, -sine_z], axis=1)
    along_z = jnp.dot(
        product.reshape(-1, NZ), table_z, precision=highest, preferred_element_type=jnp.float32
    )
    along_z = along_z.reshape(pairs_here, planes, NY, 2, NZ)
    along_y = jnp.einsum("pxyqz,yqko->pxkoz", along_z, complex_table(NY), precision=highest)
    sphere_x = sphere_index // (NY * NZ)
    sphere_y = sphere_index // NZ % NY
    sphere_z = sphere_index % NZ
    table_x = complex_table(NX)
    local_y = sphere_y - grid_index * columns
    owned_here = (local_y >= 0) & (local_y < columns)
    offsets = (sphere_x * columns + jnp.clip(local_y, 0, columns - 1)) * (2 * NZ) + sphere_z
    spectrum = jnp.einsum(
        "pxyqz,xqko->pkyoz",
        lax.all_to_all(along_y, "ga", split_axis=2, concat_axis=1, tiled=True),
        table_x,
        precision=highest,
    )
    flattened = spectrum.reshape(spectrum.shape[0], -1)
    real_part = jnp.take(flattened, offsets, axis=1)
    imag_part = jnp.take(flattened, offsets + NZ, axis=1)
    partial_value = jnp.where(owned_here[None, None, :], jnp.stack([real_part, imag_part], 1), 0.0)
    coefficient = lax.psum(partial_value, "ga") * (1.0 / math.sqrt(NX * NY * NZ))
    row_count = NG // groups
    row_block = lax.dynamic_slice_in_dim(coefficient, grid_index * row_count, row_count, 2)
    factor = 1.0 / math.sqrt(pairs_here * lax.axis_size("pair"))
    column_all = lax.all_to_all(coefficient, "pair", split_axis=2, concat_axis=0, tiled=True)
    left_side = weighted_left(
        lax.all_gather(row_block, "pair", axis=0, tiled=True),
        lax.all_gather(weights, "pair", axis=0, tiled=True),
    )
    return jnp.einsum("opqg,pqh->ogh", left_side, column_all, precision=highest) * factor


def solution(mesh):
    return jax.shard_map(
        per_device,
        mesh=mesh,
        in_specs=(P(None, None, "ga", None), P(), P("pair", None), P(), P(), P()),
        out_specs=P(None, "ga", "pair"),
        check_vma=False,
    )
```

profile of v0, /device:TPU:1, one launch (start us, length us, event | category | flops | bytes accessed | tf_op | source)
XLA Modules:
  0.0 605.0 jit_solution(15513560612721859505)
XLA Ops:
  6.5 0.8 slice_bitcast_fusion.3
  7.3 0.8 slice_bitcast_fusion.2
  8.0 0.2 select_reduce_fusion.2
  8.3 0.6 compare_and_fusion.3
  8.9 0.6 compare_and_fusion.4
  9.4 1.6 sine_negate_fusion
  11.0 0.9 fusion.27
  11.8 0.8 fusion.30
  12.7 2.2 fusion.45
  14.9 3.4 copy_bitcast_fusion
  18.3 2.3 gather_fusion
  20.6 0.0 copy-start.7
  20.6 1.6 gather_fusion.1
  22.3 0.0 copy-done.7
  22.3 3.1 convert_multiply_fusion
  25.4 2.7 reshape.135
  28.2 0.0 copy-done.1
  28.2 0.0 copy-done.2
  28.2 0.0 copy-start.3
  28.2 0.0 copy-start.4
  28.2 0.0 copy-start.5
  28.2 4.3 fusion.5
  32.5 0.0 copy-done.3
  32.5 0.0 copy-done.4
  32.5 0.0 copy-done.5
  32.6 4.7 fusion.7
  37.3 5.2 copy.77
  42.5 9.4 %all-to-all-start = ((f32[4,6,96,2,192]{4,0,3,1,2:T(4,128)}), f32[4,6,96,2,192]{4,0,3,1,2:T(4,128)}, u32[]{:S(2)}, u32[]{:S(2)}) async-start(f32[4,6,96,2,192]{4,0,3,1,2:T(4,128)} %copy.77), calls=%async_computation | async-start | bytes 9437184 | tf_op jit(solution)/shard_map/all_to_all | solution.py:70
  51.9 0.0 all-reduce.3.cloned.1.call-start
  51.9 0.0 copy-done.10
  51.9 0.6 dynamic-slice
  53.2 0.0 copy-done.8
  53.2 0.2 select_reduce_fusion
  53.4 0.1 compare_and_fusion.1
  53.5 85.7 %all-to-all-done = f32[4,6,96,2,192]{4,0,3,1,2:T(4,128)} async-done(((f32[4,6,96,2,192]{4,0,3,1,2:T(4,128)}), f32[4,6,96,2,192]{4,0,3,1,2:T(4,128)}, u32[]{:S(2)}, u32[]{:S(2)}) %all-to-all-start) | async-done | bytes 3538976 | tf_op jit(solution)/shard_map/all_to_all | solution.py:70
  139.2 4.8 copy.78
  144.0 1.7 copy.79
  145.7 5.8 fusion.10
  151.5 54.2 %copy.95 = f32[4,96,6,2,192]{0,4,3,2,1:T(8,128)} copy(f32[4,96,6,2,192]{4,1,2,0,3:T(8,128)} %fusion.10) | data formatting | bytes 7077888 | tf_op jit(solution)/shard_map/reshape | solution.py:74
  205.7 40.4 %gather_fusion.3 = f32[4096,4]{1,0:T(8,128)S(1)} fusion(f32[4,221184]{0,1:T(8,128)} %bitcast.46, s32[4096]{0:T(1024)S(1)} %get-tuple-element.17), kind=kCustom, calls=%fused_computation.3.clone | custom fusion | bytes 147456 | tf_op jit(solution)/shard_map/jit(_take)/gather | solution.py:76
  246.2 59.6 %gather_fusion.2 = f32[4096,4]{1,0:T(8,128)} fusion(f32[4,221184]{0,1:T(8,128)} %bitcast.46, s32[4096]{0:T(1024)S(1)} %get-tuple-element.16), kind=kCustom, calls=%fused_computation.1.clone | custom fusion | bytes 147456 | tf_op jit(solution)/shard_map/jit(_take)/gather | solution.py:75
  305.8 2.1 select_bitcast_fusion
  307.9 0.0 copy-done
  307.9 2.1 select_bitcast_fusion.1
  310.1 3.7 maximum_select_fusion
  313.8 0.0 all-reduce.3.cloned.1.call-update
  313.8 0.1 divide_dynamic-update-slice_fusion
  313.9 44.9 %all-reduce = f32[64]{0:T(128)S(1)} all-reduce(f32[64]{0:T(128)S(1)} %divide_dynamic-update-slice_fusion), channel_id=1, replica_groups=mesh['pair'=16,'ga'=16] {'pair'}, use_global_device_ids=true, to_apply=%add | all-reduce | flops 64 | bytes 512
  358.8 142.6 %all-reduce.3.cloned.1.call-done = f32[4,2,4096]{0,2,1:T(8,128)} async-done(((f32[4,2,4096]{0,2,1:T(8,128)}), f32[4,2,4096]{0,2,1:T(8,128)}) %all-reduce.3.cloned.1.call-update) | async-done | bytes 131088 | tf_op jit(solution)/shard_map/psum | solution.py:78
  501.4 2.5 broadcast_multiply_fusion
  504.0 16.2 %copy.111 = f32[4,2,4096]{0,1,2:T(2,128)} copy(f32[4,2,4096]{0,2,1:T(8,128)S(1)} %broadcast_multiply_fusion) | data formatting | bytes 262144 | tf_op jit(solution)/shard_map/mul | solution.py:78
  520.1 0.1 copy.84
  520.2 38.6 %all_gather.6 = f32[64,2,256]{2,1,0:T(2,128)S(1)} all-gather(f32[4,2,256]{2,1,0:T(2,128)S(1)} %copy.84), channel_id=1, replica_groups=mesh['pair'=16,'ga'=16] {'pair'}, dimensions={0}, use_global_device_ids=true | all-gather | bytes 139264 | tf_op jit(solution)/shard_map/all_gather | solution.py:84
  558.8 0.1 copy_multiply_fusion
  558.9 8.6 %reshape.147 = f32[16,1,2048]{2,1,0:T(1,128)} reshape(f32[4096,2,4]{2,1,0:T(2,128)} %bitcast.89) | data formatting | bytes 262144
  567.5 4.4 all-to-all-start.1
  571.9 0.1 fusion.49
  572.0 10.0 %all-to-all-done.1 = f32[16,1,2048]{2,1,0:T(1,128)S(1)} async-done(((f32[16,1,2048]{2,1,0:T(1,128)}), f32[16,1,2048]{2,1,0:T(1,128)S(1)}, u32[]{:S(2)}, u32[]{:S(2)}) %all-to-all-start.1) | async-done | bytes 131104 | tf_op jit(solution)/shard_map/all_to_all | solution.py:82
  581.9 0.5 broadcast.199
  582.4 0.9 reduce
  583.4 7.8 %reshape.148 = f32[4096,2,4]{2,1,0:T(2,128)} reshape(f32[16,2048]{1,0:T(8,128)S(1)} %reduce) | data formatting | bytes 262144
  591.2 5.2 copy.87
  596.5 0.1 reshape.142
  596.5 1.4 fusion.13
  (21 shorter events, 0.1 us)
Async XLA Ops:
  20.6 1.7 copy-start.7
  25.4 2.7 copy-start.1
  25.4 2.8 copy-start.2
  28.2 4.3 copy-start.3
  28.2 4.3 copy-start.4
  28.2 4.3 copy-start.5
  42.5 9.4 %copy-start.10 = (u32[256]{0:T(256)S(1)}, u32[256]{0:T(256)}, u32[]{:S(2)}) copy-start(u32[256]{0:T(256)} %constant.103) | copy-start | bytes 3076
  42.5 10.7 %copy-start.8 = (f32[8]{0:T(128)S(1)}, f32[8]{0:T(128)}, u32[]{:S(2)}) copy-start(f32[8]{0:T(128)} %param.14) | copy-start | bytes 100
  42.5 10.7 %copy-start.9 = (f32[8]{0:T(128)S(1)}, f32[8]{0:T(128)}, u32[]{:S(2)}) copy-start(f32[8]{0:T(128)} %param.13) | copy-start | bytes 100
  42.5 10.9 %copy-start.6 = (s32[4096]{0:T(1024)S(1)}, s32[4096]{0:T(1024)}, u32[]{:S(2)}) copy-start(s32[4096]{0:T(1024)} %param.15) | copy-start | bytes 49156
  42.5 96.7 %all-to-all-start = ((f32[4,6,96,2,192]{4,0,3,1,2:T(4,128)}), f32[4,6,96,2,192]{4,0,3,1,2:T(4,128)}, u32[]{:S(2)}, u32[]{:S(2)}) async-start(f32[4,6,96,2,192]{4,0,3,1,2:T(4,128)} %copy.77), calls=%async_computation | async-start | bytes 9437184 | tf_op jit(solution)/shard_map/all_to_all | solution.py:70
  51.9 449.5 %all-reduce.3.cloned.1.call-start = ((), (), s32[]{:S(2)}) async-start(), calls=%async_computation.2 | async-start | bytes 8388608 | tf_op jit(solution)/shard_map/psum | solution.py:78
  305.8 2.1 copy-start
  567.5 14.4 %all-to-all-start.1 = ((f32[16,1,2048]{2,1,0:T(1,128)}), f32[16,1,2048]{2,1,0:T(1,128)S(1)}, u32[]{:S(2)}, u32[]{:S(2)}) async-start(f32[16,1,2048]{2,1,0:T(1,128)} %reshape.147), calls=%async_computation.1 | async-start | bytes 262144 | tf_op jit(solution)/shard_map/all_to_all | solution.py:82
Sparse Core Ops, SparseCore 0:
  313.9 187.4 all-reduce.2
where the time goes:
time: 611 us; the launch traced here: 605 us
  waiting for transfers between devices  238 us (39%)
  local copies, waits for them, and re-layouts  219 us (36%)
  blocking collectives  83.5 us (14%)
  other arithmetic  19.8 us (3%)
  matrix products  16.2 us (3%)
  between operations  14.6 us (2%)
  starting transfers between devices  13.8 us (2%)
    psum x1, waiting for transfers between devices, per_device(): lax.psum(partial_value, 'ga') * (1.0 / math.sqrt(NX * NY * NZ))  143 us
    all_to_all x1, waiting for transfers between devices, per_device(): lax.all_to_all(along_y, 'ga', split_axis=2, concat_axis=1, tiled=True)  85.7 us
    gather x1, local copies, waits for them, and re-layouts, per_device(): real_part = jnp.take(flattened, offsets, axis=1)  59.6 us
    reshape x1, local copies, waits for them, and re-layouts, per_device(): flattened = spectrum.reshape(spectrum.shape[0], -1)  54.2 us
    unnamed x1, blocking collectives  44.9 us
    gather x1, local copies, waits for them, and re-layouts, per_device(): imag_part = jnp.take(flattened, offsets + NZ, axis=1)  40.4 us
    all_gather x1, blocking collectives, per_device(): lax.all_gather(row_block, 'pair', axis=0, tiled=True)  38.6 us
    unnamed x26, local copies, waits for them, and re-layouts  17 us
  transfers between devices with their start and end apart: 3, of which 3 were waited for; matrix products, arithmetic and copies ran while one was open for 0% of the time, Pallas kernels for 0%

commit v1 on v0

v1 whole, which is shorter than its diff:
```python
import math

import jax
import jax.numpy as jnp
import ml_dtypes
import numpy as np
from jax import lax
from jax.experimental import pallas as pl
from jax.experimental.pallas import tpu as pltpu
from jax.sharding import PartitionSpec as P

NX = 96
NY = 96
NZ = 192
NG = 4096
PAIRS = 64
GROUPS = 16
PLANES = NX // GROUPS
HERE = PAIRS // GROUPS
ROWS = PLANES * HERE
STEP = 4
CHUNKS = NY // STEP
WIDE = STEP * NZ
KY = 8
KZ = 16
KX = 7
BLOCK = NG // GROUPS
LOADS = 4
MESH = pl.DeviceIdType.MESH
OFFSETS = sorted(((e, d) for e in range(4) for d in range(4)), key=lambda o: -(o[0] + min(o[1], 4 - o[1])))


def split(table):
    high = table.astype(ml_dtypes.bfloat16)
    low = (table - high.astype(np.float64)).astype(ml_dtypes.bfloat16)
    return high, low


def table_along_z():
    angle = 2 * math.pi * (np.arange(NZ)[:, None] * np.arange(KZ)[None, :] % NZ) / NZ
    table = np.zeros((STEP, NZ, STEP, 2, KZ))
    for r in range(STEP):
        table[r, :, r, 0] = np.cos(angle)
        table[r, :, r, 1] = -np.sin(angle)
    return np.concatenate(split(table.reshape(WIDE, STEP * 2 * KZ)), 1)


def twiddles():
    angle = 2 * math.pi * np.arange(KY)[:, None] * np.arange(STEP)[None, :] / NY
    angle = np.repeat(angle, 2 * KZ, 1)
    return np.concatenate([np.cos(angle), np.sin(angle)]).astype(np.float32)


def table_along_x():
    table = np.zeros((GROUPS, 2, PLANES, HERE, 256))
    for j in range(GROUPS):
        for x in range(PLANES):
            for f in range(-KX, KX + 1):
                angle = 2 * math.pi * (f * (PLANES * j + x) % NX) / NX
                table[j, 0, x, :, 16 + f + KX] = math.cos(angle)
                table[j, 1, x, :, 16 + f + KX] = math.sin(angle)
    high, low = split(table.reshape(GROUPS, 2 * ROWS, 256))
    return np.concatenate([high, low], 1)


def halves(value):
    high = value.astype(jnp.bfloat16)
    return high, (value - high.astype(jnp.float32)).astype(jnp.bfloat16)


def dot(left, right):
    return jnp.dot(left, right, preferred_element_type=jnp.float32)


def rem(value, size):
    return lax.rem(value, size)


def coefficients_kernel(
    owner_in, pairs_in, energy_v_in, energy_c_in, sphere_in, orbitals, table_z, table_y, table_x, rows, cols,
    owner, pairs, energy_v, energy_c, sphere, orb, tz, ty, tx, high_ref, low_ref, along_z, hot, left, part, landed, total,
    sems, send1, recv1, send_col, recv_col, send_row, recv_row, send_fc, recv_fc, send_fr, recv_fr,
):
    i, j = lax.axis_index("pair"), lax.axis_index("ga")
    zh, y, core = i // 8, rem(i // 2, 4), rem(i, 2)
    zl, x = j // 4, rem(j, 4)
    sibling = i + 1 - 2 * core

    def pair_at(zh, y, core):
        return zh * 8 + rem(y, 4) * 2 + core

    def ga_at(zl, x):
        return rem(zl, 4) * 4 + rem(x, 4)

    mine = ga_at(zl + 2, x + 4 - y)
    own = mine == i
    col_y = rem(x + 4 - rem(i, 4), 4)

    moves = (
        (owner_in, owner), (pairs_in, pairs), (energy_v_in, energy_v), (energy_c_in, energy_c), (sphere_in, sphere),
        (table_z, tz), (table_x.at[j], tx), (table_y, ty),
    )
    copies = [pltpu.make_async_copy(source, target, sems.at[LOADS + n]) for n, (source, target) in enumerate(moves)]
    loads = []
    span = CHUNKS // LOADS * WIDE
    for n in range(LOADS):
        lanes = pl.ds(n * span, span)
        loads.append(pltpu.make_async_copy(orbitals.at[:, lanes], orb.at[:, lanes], sems.at[n]))
    for copy in copies[4:5] + loads[:1] + copies[:4] + copies[5:6] + loads[1:] + copies[6:]:
        copy.start()

    barrier = pltpu.get_barrier_semaphore()

    def greet(device):
        pl.semaphore_signal(barrier, inc=1, device_id=device, device_id_type=MESH)

    turn = jnp.where(zl < 2, 1, 3)
    for e, d in OFFSETS[:-1]:
        greet((i, ga_at(zl + turn * e, x + d)))
    across = ga_at(jnp.where(zl < 2, 3, 0), x)
    for d in (2, 1, 3, 0):
        greet((pair_at(1 - zh, y + d, core), across))
    greet((pair_at(1 - zh, col_y, 1 - core), across))
    for d in (2, 1, 3):
        greet((pair_at(zh, y + d, core), j))
    greet((pair_at(zh, col_y, 1 - core), j))
    greet((sibling, j))
    side = jnp.where(rem(zl, 3) == 0, 1, 0)
    even = 1 - rem(x + 4 - (1 - core) + y, 2)
    greeted = (GROUPS - 1) + 4 + 8 * side + even * (2 + 4 * side)

    copies[4].wait()
    position = sphere[...]
    column = lax.shift_right_logical(lax.shift_right_logical(position, 6) * 43691, 17)
    index_z = position - column * NZ
    index_x = lax.shift_right_logical(lax.shift_right_logical(column, 5) * 43691, 17)
    index_y = column - index_x * NY
    freq_x = jnp.where(index_x >= NX // 2, index_x - NX, index_x)
    freq_y = jnp.where(index_y >= NY // 2, index_y - NY, index_y)
    freq_z = jnp.where(index_z >= NZ // 2, index_z - NZ, index_z)
    flip = freq_z < 0
    freq_x = jnp.where(flip, -freq_x, freq_x) + KX
    freq_y = jnp.where(flip, -freq_y, freq_y)
    mode = jnp.abs(freq_y) * 32 + jnp.where(freq_y < 0, 16, 0) + jnp.abs(freq_z)
    sign = jnp.where(flip, -1.0, 1.0)
    row = lax.broadcasted_iota(jnp.int32, (256, BLOCK), 0)
    for b in range(GROUPS):
        lanes = slice(b * BLOCK, (b + 1) * BLOCK)
        hot[b, :256] = jnp.where(row == mode[:, lanes], 1.0, 0.0).astype(jnp.bfloat16)
        hot[b, 16:32] = jnp.where(row[:16] == freq_x[:, lanes], 1.0, 0.0).astype(jnp.bfloat16)
        hot[b, 256:] = jnp.broadcast_to(sign[:, lanes], (16, BLOCK)).astype(jnp.bfloat16)

    for copy in copies[:4]:
        copy.wait()
    place = rem(lax.broadcasted_iota(jnp.int32, (8, WIDE), 0), HERE)
    slot_v = jnp.zeros((8, WIDE), jnp.int32)
    slot_c = jnp.zeros((8, WIDE), jnp.int32)
    gap = jnp.zeros((8, BLOCK), jnp.float32)
    for p in range(HERE):
        v, c = pairs[0, p], pairs[1, p]
        slot_v = jnp.where(place == p, owner[0, v], slot_v)
        slot_c = jnp.where(place == p, owner[1, c], slot_c)
        gap = jnp.where(place[:, :BLOCK] == p, energy_c[c] - energy_v[v], gap)
    scale = jnp.sqrt(2.0 / gap) * (1.0 / math.sqrt(NX * NY * NZ * math.sqrt(PAIRS)))

    upper = lax.broadcasted_iota(jnp.int32, (8, WIDE), 0) < HERE

    def pick(value, slots):
        return jnp.take_along_axis(value, slots, axis=0, mode="promise_in_bounds")

    copies[5].wait()
    group = CHUNKS // LOADS
    for n in range(LOADS):
        loads[n].wait()

        @pl.loop(n * group // 2, (n + 1) * group // 2, unroll=True)
        def _(u):
            values = []
            for s in range(2):
                lanes = pl.ds(pl.multiple_of((2 * u + s) * WIDE, 128), WIDE)
                for a in range(PLANES // 2):
                    val = orb[16 * a : 16 * a + 16, lanes].astype(jnp.float32)
                    con = orb[48 + 16 * a : 64 + 16 * a, lanes].astype(jnp.float32)
                    first = pick(val[:8], slot_v) * pick(con[:8], slot_c)
                    second = pick(val[8:], slot_v) * pick(con[8:], slot_c)
                    values.append(jnp.where(upper, first, second))
            high, low = halves(jnp.concatenate(values, 0))
            here = pl.ds(pl.multiple_of(u * 2 * ROWS, 16), 2 * ROWS)
            high_ref[here] = high
            low_ref[here] = low

        here = slice(n * group * ROWS, (n + 1) * group * ROWS)
        result = dot(high_ref[here], tz[...]) + dot(low_ref[here], tz[...])
        result = result[:, :128] + result[:, 128:]
        along_z[n * group : (n + 1) * group] = result.reshape(group, ROWS, 128)

    for copy in copies[6:]:
        copy.wait()
    lane = lax.broadcasted_iota(jnp.int32, (8, 128), 1)
    real_lane = rem(lane, 2 * KZ) < KZ
    turn_sign = jnp.where(real_lane, 1.0, -1.0)
    modes = [[], []]
    for a in range(ROWS // 8):
        here = slice(a * 8, a * 8 + 8)
        first, middle = along_z[0, here], along_z[CHUNKS // 2, here]
        even, odd = [], []
        for t in range(1, CHUNKS // 2):
            one, other = along_z[t, here], along_z[CHUNKS - t, here]
            even.append(one + other)
            odd.append(one - other)
        placed = [[None, None], [None, None]]
        for k in range(KY):
            total_cos = first + middle if k % 2 == 0 else first - middle
            total_sin = None
            for t in range(1, CHUNKS // 2):
                angle = 2 * math.pi * (k * t % CHUNKS) / CHUNKS
                total_cos = total_cos + even[t - 1] * math.cos(angle)
                term = odd[t - 1] * math.sin(angle)
                total_sin = term if total_sin is None else total_sin + term
            cosine, sine = ty[k : k + 1], ty[KY + k : KY + k + 1]
            same = cosine * total_cos - sine * total_sin
            cross = sine * total_cos + cosine * total_sin
            for shift in (2 * KZ, 4 * KZ):
                same = same + pltpu.roll(same, shift, 1)
                cross = cross + pltpu.roll(cross, shift, 1)
            cross = pltpu.roll(cross, KZ, 1) * turn_sign
            plus, minus = same + cross, same - cross
            real = jnp.where(real_lane, plus, pltpu.roll(minus, KZ, 1))
            imag = jnp.where(real_lane, pltpu.roll(plus, KZ, 1), minus)
            if k == 0:
                real, imag = jnp.where(real_lane, real, 0.0), jnp.where(real_lane, imag, 0.0)
            spot = lane // (2 * KZ) == k % 4
            for c, value in enumerate((real, imag)):
                old = placed[c][k // 4]
                placed[c][k // 4] = value if old is None else jnp.where(spot, value, old)
        for c in range(2):
            modes[c].append(jnp.concatenate(placed[c], 1))
    high, low = halves(jnp.concatenate(modes[0] + modes[1], 0))
    left[: 2 * ROWS] = high
    left[2 * ROWS : 4 * ROWS] = low
    left[4 * ROWS :] = tx[...]

    pl.semaphore_wait(barrier, greeted)
    upper = upper[:, :BLOCK]

    def to_group(n, slot, peer):
        return pltpu.make_async_remote_copy(
            part.at[n], landed.at[slot], send1.at[n], recv1.at[slot], device_id=(i, peer), device_id_type=MESH
        )

    sent = []
    for n, (e, d) in enumerate(OFFSETS):
        peer = ga_at(zl + turn * e, x + d)
        block = ga_at(zl + turn * e + 2, x + d + 4 - y)
        picked = dot(left[...], hot[block, :256])
        real = imag = jnp.zeros((8, BLOCK), jnp.float32)
        for a in range(ROWS // 8):
            re, im, cosine, sine = [
                picked[s * ROWS + a * 8 : s * ROWS + a * 8 + 8]
                + picked[s * ROWS + lag * ROWS + a * 8 : s * ROWS + lag * ROWS + a * 8 + 8]
                for s, lag in ((0, 2), (1, 2), (4, 2), (5, 2))
            ]
            real = real + cosine * re + sine * im
            imag = imag + cosine * im - sine * re
        imag = imag * hot[block, 256:].astype(jnp.float32)[:8]
        real = real + pltpu.roll(real, HERE, 0)
        imag = imag + pltpu.roll(imag, HERE, 0)
        part[n] = jnp.where(upper, real, imag) * scale
        if n < GROUPS - 1:
            copy = to_group(n, j, peer)
            copy.start()
            sent.append(copy)

    value = part[GROUPS - 1]
    for n, (e, d) in reversed(list(enumerate(OFFSETS[:-1]))):
        peer = ga_at(zl + turn * e, x + d)
        to_group(n, peer, peer).wait_recv()
        value = value + landed[peer]
    total[...] = value

    def col_slot(zh, y, core):
        return y * 4 + zh * 2 + core

    def row_slot(zh, y, core):
        return core * 8 + y * 2 + zh

    def col_copy(n, to_z, h, s):
        return pltpu.make_async_remote_copy(
            total, cols.at[s], send_col.at[n], recv_col.at[h], device_id=(mine, ga_at(to_z, x)), device_id_type=MESH
        )

    my_col = col_slot(zh, y, core)
    lift = jnp.where(mine // 8 == zh, 2, 0)

    @pl.when(own)
    def _():
        cols[my_col] = total[...]

    for n, d in enumerate((0, 1, 3, 2)):
        to_z = rem(zl + lift + d, 4)

        @pl.when(jnp.logical_not(jnp.logical_and(own, to_z == zl)))
        def _():
            col_copy(n, to_z, zh * 2 + core, my_col).start()

    def row_copy(n, to_h, to_y, h, s):
        return pltpu.make_async_remote_copy(
            total, rows.at[s], send_row.at[n], recv_row.at[h],
            device_id=(pair_at(to_h, to_y, core), mine), device_id_type=MESH,
        )

    my_row = row_slot(zh, y, core)
    targets = [(h, d) for d in (2, 1, 3, 0) for h in range(2)]
    for n, (h, d) in enumerate(targets):
        row_copy(n, h, y + d, y * 2 + zh, my_row).start()

    def pass_col(n, d, slot, sem):
        two = cols.at[pl.ds(slot, 2)]
        return pltpu.make_async_remote_copy(
            two, two, send_fc.at[n], recv_fc.at[sem], device_id=(i, ga_at(zl, x + d)), device_id_type=MESH
        )

    for step in range(2):
        h = zh if step == 0 else 1 - zh
        for c in range(2):
            self_sent = jnp.logical_and(own, jnp.logical_and(h == zh, core == c))

            @pl.when(jnp.logical_not(self_sent))
            def _():
                col_copy(0, zl, h * 2 + c, col_slot(h, col_y, c)).wait_recv()

        for n, d in enumerate((2, 1, 3)):
            pass_col(step * 3 + n, d, col_slot(h, col_y, 0), col_y * 2 + h).start()

    def pass_row(n, y, c):
        two = rows.at[pl.ds(row_slot(0, y, c), 2)]
        return pltpu.make_async_remote_copy(
            two, two, send_fr.at[n], recv_fr.at[y], device_id=(sibling, j), device_id_type=MESH
        )

    for n, d in enumerate((0, 1, 3, 2)):
        from_y = rem(y + d, 4)
        for h in range(2):
            row_copy(0, h, from_y, from_y * 2 + h, row_slot(h, from_y, core)).wait_recv()
        pass_row(n, from_y, core).start()

    for copy in sent:
        copy.wait_send()
    for n, d in enumerate((0, 1, 3, 2)):
        to_z = rem(zl + lift + d, 4)

        @pl.when(jnp.logical_not(jnp.logical_and(own, to_z == zl)))
        def _():
            col_copy(n, to_z, zh * 2 + core, my_col).wait_send()

    for n, (h, d) in enumerate(targets):
        row_copy(n, h, y + d, y * 2 + zh, my_row).wait_send()
    for n, d in enumerate((0, 1, 3, 2)):
        from_y = rem(y + d, 4)
        pass_row(n, from_y, core).wait_send()
        pass_row(n, from_y, 1 - core).wait_recv()
    for step in range(2):
        h = zh if step == 0 else 1 - zh
        for n, d in enumerate((2, 1, 3)):
            pass_col(step * 3 + n, d, col_slot(h, col_y, 0), col_y * 2 + h).wait_send()
            from_y = rem(col_y + d, 4)
            pass_col(0, d, col_slot(h, from_y, 0), from_y * 2 + h).wait_recv()


def coefficients(owner, pairs, energy_v, energy_c, sphere, orbitals):
    vmem = pl.BlockSpec(memory_space=pltpu.VMEM)
    hbm = pl.BlockSpec(memory_space=pl.ANY)
    points = NY * NZ
    block = jax.ShapeDtypeStruct((GROUPS, 8, BLOCK), jnp.float32)
    dma = pltpu.SemaphoreType.DMA
    return pl.pallas_call(
        coefficients_kernel,
        out_shape=(block, block),
        in_specs=[hbm] * 9,
        out_specs=(vmem, vmem),
        scratch_shapes=[
            pltpu.SMEM((2, 8), jnp.int32),
            pltpu.SMEM((2, HERE), jnp.int32),
            pltpu.SMEM((8,), jnp.float32),
            pltpu.SMEM((8,), jnp.float32),
            pltpu.VMEM((1, NG), jnp.int32),
            pltpu.VMEM((16 * PLANES, points), jnp.bfloat16),
            pltpu.VMEM((WIDE, 256), jnp.bfloat16),
            pltpu.VMEM((2 * KY, 128), jnp.float32),
            pltpu.VMEM((4 * ROWS, 256), jnp.bfloat16),
            pltpu.VMEM((CHUNKS * ROWS, WIDE), jnp.bfloat16),
            pltpu.VMEM((CHUNKS * ROWS, WIDE), jnp.bfloat16),
            pltpu.VMEM((CHUNKS, ROWS, 128), jnp.float32),
            pltpu.VMEM((GROUPS, 256 + 16, BLOCK), jnp.bfloat16),
            pltpu.VMEM((8 * ROWS, 256), jnp.bfloat16),
            pltpu.VMEM((GROUPS, 8, BLOCK), jnp.float32),
            pltpu.VMEM((GROUPS, 8, BLOCK), jnp.float32),
            pltpu.VMEM((8, BLOCK), jnp.float32),
            dma((LOADS + 8,)), dma((GROUPS,)), dma((GROUPS,)), dma((4,)), dma((4,)), dma((8,)), dma((8,)),
            dma((6,)), dma((8,)), dma((4,)), dma((4,)),
        ],
        compiler_params=pltpu.CompilerParams(
            collective_id=0, has_side_effects=True, vmem_limit_bytes=56 * 1024 * 1024
        ),
        name="coefficients",
    )(
        owner, pairs.T, energy_v, energy_c, sphere.reshape(1, NG),
        orbitals.transpose(0, 2, 1, 3).reshape(16 * PLANES, points),
        jnp.asarray(table_along_z()), jnp.asarray(twiddles()), jnp.asarray(table_along_x()),
    )


def outer_kernel(rows, cols, out, result, sems):
    order = [c * 8 + y * 2 + h for y in range(4) for h in range(2) for c in range(2)]
    left = jnp.concatenate([rows[n] for n in order], 0)
    left_high, left_low = halves(left)
    left = jnp.concatenate([left_high, left_high, left_low], 0)
    blocks = -cols[...]
    swapped = jnp.concatenate([-blocks[:, HERE:], blocks[:, :HERE]], 1)
    right = jnp.concatenate([v.reshape(PAIRS * 2, BLOCK) for v in (blocks, swapped)], 1)
    right_high, right_low = halves(right)
    right = jnp.concatenate([right_high, right_low, right_high], 0)
    turned = left.T
    copies = []
    for n in range(2):
        here = pl.ds(n * 128, 128)
        value = dot(turned[n * 128 : n * 128 + 128], right)
        result[0, here] = value[:, :BLOCK]
        result[1, here] = value[:, BLOCK:]
        copies.append(pltpu.make_async_copy(result.at[:, here], out.at[:, here], sems.at[n]))
        copies[-1].start()
    for copy in copies:
        copy.wait()


def outer(rows, cols):
    vmem = pl.BlockSpec(memory_space=pltpu.VMEM)
    return pl.pallas_call(
        outer_kernel,
        out_shape=jax.ShapeDtypeStruct((2, BLOCK, BLOCK), jnp.float32),
        in_specs=[vmem, vmem],
        out_specs=pl.BlockSpec(memory_space=pl.ANY),
        scratch_shapes=[pltpu.VMEM((2, BLOCK, BLOCK), jnp.float32), pltpu.SemaphoreType.DMA((2,))],
        name="outer",
    )(rows, cols)


def per_device(orbitals, owner, pair_list, valence_energy, conduction_energy, sphere_index):
    rows, cols = coefficients(owner, pair_list, valence_energy, conduction_energy, sphere_index, orbitals)
    return outer(rows, cols)


def solution(mesh):
    return jax.shard_map(
        per_device,
        mesh=mesh,
        in_specs=(P(None, None, "ga", None), P(), P("pair", None), P(), P(), P()),
        out_specs=P(None, "ga", "pair"),
        check_vma=False,
    )
```

time: 611 us -> 28.7 us (0.05)
  waiting for transfers between devices: 238 us -> 0 us
  local copies, waits for them, and re-layouts: 219 us -> 0 us
  blocking collectives: 83.5 us -> 0 us
  Pallas kernels: 0 us -> 28.5 us
  other arithmetic: 19.8 us -> 0 us
  matrix products: 16.2 us -> 0 us
  between operations: 14.6 us -> 0.01 us
  starting transfers between devices: 13.8 us -> 0 us
    psum x1 -> x0, waiting for transfers between devices: 143 us -> none  [per_device(): lax.psum(partial_value, 'ga') * (1.0 / math.sqrt(NX * NY * NZ))]
    gather x4 -> x0, local copies, waits for them, and re-layouts: 104 us -> none  [the longest x1 59.6 us: per_device(): real_part = jnp.take(flattened, offsets, axis=1)]
    all_to_all x2 -> x0, waiting for transfers between devices: 95.7 us -> none  [the longest x1 85.7 us: per_device(): lax.all_to_all(along_y, 'ga', split_axis=2, concat_axis=1, tiled=True)]
    reshape x1 -> x0, local copies, waits for them, and re-layouts: 54.2 us -> none  [per_device(): flattened = spectrum.reshape(spectrum.shape[0], -1)]
    unnamed x1 -> x0, blocking collectives: 44.9 us -> none
    all_gather x1 -> x0, blocking collectives: 38.6 us -> none  [per_device(): lax.all_gather(row_block, 'pair', axis=0, tiled=True)]
    pallas_call x0 -> x2, Pallas kernels: none -> 28.5 us  [the longest x1 26.5 us: coefficients(): pl.pallas_call(coefficients_kernel, out_shape=(block, block), in_specs=[h...]
    unnamed x26 -> x0, local copies, waits for them, and re-layouts: 17 us -> none
  transfers between devices with their start and end apart: 3 -> 0, of which waited for: 3 -> 0; matrix products, arithmetic and copies ran while one was open for 0% -> 0% of each run, Pallas kernels for 0% -> 0%
where the time goes in v1:
time: 28.7 us; the launch traced here: 28.5 us
  Pallas kernels  28.5 us (99%)
    pallas_call x1, Pallas kernels, coefficients(): pl.pallas_call(coefficients_kernel, out_shape=(block, block), in_specs=[h...  26.5 us
    pallas_call x1, Pallas kernels, outer(): pl.pallas_call(outer_kernel, out_shape=jax.ShapeDtypeStruct((2, BLOCK, BL...  2.03 us

profile of v1, /device:TPU:1, one launch (start us, length us, event | category | flops | bytes accessed | tf_op | source)
XLA Modules:
  0.0 28.5 jit_solution(15256761448577487795)
XLA Ops:
  0.0 26.5 %coefficients.1 = (f32[16,8,256]{2,1,0:T(8,128)}, f32[16,8,256]{2,1,0:T(8,128)}) custom-call(s32[2,8]{1,0:T(2,128)} %owner_in.1, s32[2,4]{1,0:T(2,128)} %bitcast.7, f32[8]{0:T(128)} %energy_v_in.1, f32[8]{0:T(128)} %energy_c_in.1, s32[1,4096]{1,0:T(1,128)} %bitcast.6, bf16[96,18432]{1,0:T(8,128)(2,1)} %bitcast.5, bf16[768,256]{1,0:T(8,128)(2,1)} %constant.6.clone.table_z, ...), custom_call_target="tpu_custom_call" | custom-call | tf_op jit(solution)/shard_map/coefficients/pallas_call | solution.py:376
  26.5 2.0 %outer.1 = f32[2,256,256]{2,1,0:T(8,128)} custom-call(f32[16,8,256]{2,1,0:T(8,128)} %get-tuple-element.7.rows, f32[16,8,256]{2,1,0:T(8,128)} %get-tuple-element.8.cols), custom_call_target="tpu_custom_call" | custom-call | tf_op jit(solution)/shard_map/outer/pallas_call | solution.py:438

commit v2 on v1

--- a/solution.py
+++ b/solution.py
@@ -77,9 +77,9 @@
 
 
 def coefficients_kernel(
-    owner_in, pairs_in, energy_v_in, energy_c_in, sphere_in, orbitals, table_z, table_y, table_x, rows, cols,
+    owner_in, pairs_in, energy_v_in, energy_c_in, sphere_in, orbitals, table_z, table_y, table_x, out,
     owner, pairs, energy_v, energy_c, sphere, orb, tz, ty, tx, high_ref, low_ref, along_z, hot, left, part, landed, total,
-    sems, send1, recv1, send_col, recv_col, send_row, recv_row, send_fc, recv_fc, send_fr, recv_fr,
+    rows, cols, sems, send1, recv1, send_col, recv_col, send_row, recv_row, send_fc, recv_fc, send_fr, recv_fr,
 ):
     i, j = lax.axis_index("pair"), lax.axis_index("ga")
     zh, y, core = i // 8, rem(i // 2, 4), rem(i, 2)
@@ -279,10 +279,10 @@
     total[...] = value
 
     def col_slot(zh, y, core):
-        return y * 4 + zh * 2 + core
+        return zh * 8 + y * 2 + core
 
     def row_slot(zh, y, core):
-        return core * 8 + y * 2 + zh
+        return zh * 8 + core * 4 + y
 
     def col_copy(n, to_z, h, s):
         return pltpu.make_async_remote_copy(
@@ -320,8 +320,19 @@
             two, two, send_fc.at[n], recv_fc.at[sem], device_id=(i, ga_at(zl, x + d)), device_id_type=MESH
         )
 
-    for step in range(2):
-        h = zh if step == 0 else 1 - zh
+    def pass_row(h, c):
+        four = rows.at[pl.ds(row_slot(h, 0, c), 4)]
+        return pltpu.make_async_remote_copy(
+            four, four, send_fr.at[h], recv_fr.at[h], device_id=(sibling, j), device_id_type=MESH
+        )
+
+    def wait_rows(h):
+        for d in (0, 1, 3, 2):
+            from_y = rem(y + d, 4)
+            row_copy(0, h, from_y, from_y * 2 + h, row_slot(h, from_y, core)).wait_recv()
+        pass_row(h, core).start()
+
+    def wait_cols(step, h):
         for c in range(2):
             self_sent = jnp.logical_and(own, jnp.logical_and(h == zh, core == c))
 
@@ -332,17 +343,10 @@
         for n, d in enumerate((2, 1, 3)):
             pass_col(step * 3 + n, d, col_slot(h, col_y, 0), col_y * 2 + h).start()
 
-    def pass_row(n, y, c):
-        two = rows.at[pl.ds(row_slot(0, y, c), 2)]
-        return pltpu.make_async_remote_copy(
-            two, two, send_fr.at[n], recv_fr.at[y], device_id=(sibling, j), device_id_type=MESH
-        )
-
-    for n, d in enumerate((0, 1, 3, 2)):
-        from_y = rem(y + d, 4)
-        for h in range(2):
-            row_copy(0, h, from_y, from_y * 2 + h, row_slot(h, from_y, core)).wait_recv()
-        pass_row(n, from_y, core).start()
+    halfs = (zh, 1 - zh)
+    for step, h in enumerate(halfs):
+        wait_cols(step, h)
+        wait_rows(h)
 
     for copy in sent:
         copy.wait_send()
@@ -355,29 +359,35 @@
 
     for n, (h, d) in enumerate(targets):
         row_copy(n, h, y + d, y * 2 + zh, my_row).wait_send()
-    for n, d in enumerate((0, 1, 3, 2)):
-        from_y = rem(y + d, 4)
-        pass_row(n, from_y, core).wait_send()
-        pass_row(n, from_y, 1 - core).wait_recv()
-    for step in range(2):
-        h = zh if step == 0 else 1 - zh
+
+    for step, h in enumerate(halfs):
+        pass_row(h, core).wait_send()
+        pass_row(h, 1 - core).wait_recv()
+        high, low = halves(jnp.concatenate([rows[h * 8 + c * 4 + y] for y in range(4) for c in range(2)], 0).T)
+        turned = jnp.concatenate([high, high, low], 1)
         for n, d in enumerate((2, 1, 3)):
             pass_col(step * 3 + n, d, col_slot(h, col_y, 0), col_y * 2 + h).wait_send()
+        for n, d in enumerate((1, 3, 2)):
             from_y = rem(col_y + d, 4)
             pass_col(0, d, col_slot(h, from_y, 0), from_y * 2 + h).wait_recv()
+        blocks = -cols[pl.ds(h * 8, 8)]
+        swapped = jnp.concatenate([-blocks[:, HERE:], blocks[:, :HERE]], 1)
+        for o, value in enumerate((blocks, swapped)):
+            high, low = halves(value.reshape(PAIRS, BLOCK))
+            value = dot(turned, jnp.concatenate([high, low, high], 0))
+            out[o] = value if step == 0 else out[o] + value
 
 
 def coefficients(owner, pairs, energy_v, energy_c, sphere, orbitals):
     vmem = pl.BlockSpec(memory_space=pltpu.VMEM)
     hbm = pl.BlockSpec(memory_space=pl.ANY)
     points = NY * NZ
-    block = jax.ShapeDtypeStruct((GROUPS, 8, BLOCK), jnp.float32)
     dma = pltpu.SemaphoreType.DMA
     return pl.pallas_call(
         coefficients_kernel,
-        out_shape=(block, block),
+        out_shape=jax.ShapeDtypeStruct((2, BLOCK, BLOCK), jnp.float32),
         in_specs=[hbm] * 9,
-        out_specs=(vmem, vmem),
+        out_specs=vmem,
         scratch_shapes=[
             pltpu.SMEM((2, 8), jnp.int32),
             pltpu.SMEM((2, HERE), jnp.int32),
@@ -396,58 +406,27 @@
             pltpu.VMEM((GROUPS, 8, BLOCK), jnp.float32),
             pltpu.VMEM((GROUPS, 8, BLOCK), jnp.float32),
             pltpu.VMEM((8, BLOCK), jnp.float32),
+            pltpu.VMEM((GROUPS, 8, BLOCK), jnp.float32),
+            pltpu.VMEM((GROUPS, 8, BLOCK), jnp.float32),
             dma((LOADS + 8,)), dma((GROUPS,)), dma((GROUPS,)), dma((4,)), dma((4,)), dma((8,)), dma((8,)),
-            dma((6,)), dma((8,)), dma((4,)), dma((4,)),
+            dma((6,)), dma((8,)), dma((2,)), dma((2,)),
         ],
         compiler_params=pltpu.CompilerParams(
-            collective_id=0, has_side_effects=True, vmem_limit_bytes=56 * 1024 * 1024
+            collective_id=0, has_side_effects=True, vmem_limit_bytes=40 * 1024 * 1024
         ),
         name="coefficients",
-    )(
-        owner, pairs.T, energy_v, energy_c, sphere.reshape(1, NG),
-        orbitals.transpose(0, 2, 1, 3).reshape(16 * PLANES, points),
-        jnp.asarray(table_along_z()), jnp.asarray(twiddles()), jnp.asarray(table_along_x()),
-    )
-
-
-def outer_kernel(rows, cols, out, result, sems):
-    order = [c * 8 + y * 2 + h for y in range(4) for h in range(2) for c in range(2)]
-    left = jnp.concatenate([rows[n] for n in order], 0)
-    left_high, left_low = halves(left)
-    left = jnp.concatenate([left_high, left_high, left_low], 0)
-    blocks = -cols[...]
-    swapped = jnp.concatenate([-blocks[:, HERE:], blocks[:, :HERE]], 1)
-    right = jnp.concatenate([v.reshape(PAIRS * 2, BLOCK) for v in (blocks, swapped)], 1)
-    right_high, right_low = halves(right)
-    right = jnp.concatenate([right_high, right_low, right_high], 0)
-    turned = left.T
-    copies = []
-    for n in range(2):
-        here = pl.ds(n * 128, 128)
-        value = dot(turned[n * 128 : n * 128 + 128], right)
-        result[0, here] = value[:, :BLOCK]
-        result[1, here] = value[:, BLOCK:]
-        copies.append(pltpu.make_async_copy(result.at[:, here], out.at[:, here], sems.at[n]))
-        copies[-1].start()
-    for copy in copies:
-        copy.wait()
-
-
-def outer(rows, cols):
-    vmem = pl.BlockSpec(memory_space=pltpu.VMEM)
-    return pl.pallas_call(
-        outer_kernel,
-        out_shape=jax.ShapeDtypeStruct((2, BLOCK, BLOCK), jnp.float32),
-        in_specs=[vmem, vmem],
-        out_specs=pl.BlockSpec(memory_space=pl.ANY),
-        scratch_shapes=[pltpu.VMEM((2, BLOCK, BLOCK), jnp.float32), pltpu.SemaphoreType.DMA((2,))],
-        name="outer",
-    )(rows, cols)
+    )(*[
+        pltpu.with_memory_space_constraint(value, pltpu.HBM)
+        for value in (
+            owner, pairs.T, energy_v, energy_c, sphere.reshape(1, NG),
+            orbitals.transpose(0, 2, 1, 3).reshape(16 * PLANES, points),
+            jnp.asarray(table_along_z()), jnp.asarray(twiddles()), jnp.asarray(table_along_x()),
+        )
+    ])
 
 
 def per_device(orbitals, owner, pair_list, valence_energy, conduction_energy, sphere_index):
-    rows, cols = coefficients(owner, pair_list, valence_energy, conduction_energy, sphere_index, orbitals)
-    return outer(rows, cols)
+    return coefficients(owner, pair_list, valence_energy, conduction_energy, sphere_index, orbitals)
 
 
 def solution(mesh):

time: 28.7 us -> 27.1 us (0.944)
  Pallas kernels: 28.5 us -> 26.2 us
  local copies, waits for them, and re-layouts: 0 us -> 0.8 us
    pallas_call x2 -> x1, Pallas kernels: 28.5 us -> 26.2 us  [coefficients(): pl.pallas_call(coefficients_kernel, out_shape=jax.ShapeDtypeStruct((2, BL...]
    unnamed x0 -> x1, local copies, waits for them, and re-layouts: none -> 0.8 us
where the time goes in v2:
time: 27.1 us; the launch traced here: 27 us
  Pallas kernels  26.2 us (97%)
  local copies, waits for them, and re-layouts  0.8 us (3%)
    pallas_call x1, Pallas kernels, coefficients(): pl.pallas_call(coefficients_kernel, out_shape=jax.ShapeDtypeStruct((2, BL...  26.2 us
    unnamed x1, local copies, waits for them, and re-layouts  0.8 us

profile of v2, /device:TPU:1, one launch (start us, length us, event | category | flops | bytes accessed | tf_op | source)
XLA Modules:
  0.0 27.0 jit_solution(1512356356548347836)
XLA Ops:
  0.0 26.2 %coefficients.1 = f32[2,256,256]{2,1,0:T(8,128)S(1)} custom-call(s32[2,8]{1,0:T(2,128)} %owner_in.1, s32[2,4]{1,0:T(2,128)} %bitcast.7, f32[8]{0:T(128)} %energy_v_in.1, f32[8]{0:T(128)} %energy_c_in.1, s32[1,4096]{1,0:T(1,128)} %bitcast.6, bf16[96,18432]{1,0:T(8,128)(2,1)} %bitcast.5, bf16[768,256]{1,0:T(8,128)(2,1)} %constant.6.clone.table_z, ...), custom_call_target="tpu_custom_call" | custom-call | tf_op jit(solution)/shard_map/coefficients/pallas_call | solution.py:386
  26.2 0.8 %copy.11 = f32[2,256,256]{2,1,0:T(8,128)} copy(f32[2,256,256]{2,1,0:T(8,128)S(1)} %coefficients.1) | data formatting | bytes 1048576

commit v3 on v2

--- a/solution.py
+++ b/solution.py
@@ -92,9 +92,15 @@
     def ga_at(zl, x):
         return rem(zl, 4) * 4 + rem(x, 4)
 
-    mine = ga_at(zl + 2, x + 4 - y)
+    def mix(a, b):
+        return rem(a // 2 + b // 2, 2) * 2 + rem(a + b, 2)
+
+    def block_at(zl, x):
+        return mix(rem(zl + 2, 4), rem(y, 2)) * 4 + mix(x, y)
+
+    mine = block_at(zl, x)
     own = mine == i
-    col_y = rem(x + 4 - rem(i, 4), 4)
+    col_y = mix(x, rem(i, 4))
 
     moves = (
         (owner_in, owner), (pairs_in, pairs), (energy_v_in, energy_v), (energy_c_in, energy_c), (sphere_in, sphere),
@@ -126,7 +132,7 @@
     greet((pair_at(zh, col_y, 1 - core), j))
     greet((sibling, j))
     side = jnp.where(rem(zl, 3) == 0, 1, 0)
-    even = 1 - rem(x + 4 - (1 - core) + y, 2)
+    even = rem(x + y + core, 2)
     greeted = (GROUPS - 1) + 4 + 8 * side + even * (2 + 4 * side)
 
     copies[4].wait()
@@ -170,29 +176,35 @@
 
     copies[5].wait()
     group = CHUNKS // LOADS
-    for n in range(LOADS):
-        loads[n].wait()
-
-        @pl.loop(n * group // 2, (n + 1) * group // 2, unroll=True)
-        def _(u):
-            values = []
-            for s in range(2):
-                lanes = pl.ds(pl.multiple_of((2 * u + s) * WIDE, 128), WIDE)
-                for a in range(PLANES // 2):
-                    val = orb[16 * a : 16 * a + 16, lanes].astype(jnp.float32)
-                    con = orb[48 + 16 * a : 64 + 16 * a, lanes].astype(jnp.float32)
-                    first = pick(val[:8], slot_v) * pick(con[:8], slot_c)
-                    second = pick(val[8:], slot_v) * pick(con[8:], slot_c)
-                    values.append(jnp.where(upper, first, second))
-            high, low = halves(jnp.concatenate(values, 0))
-            here = pl.ds(pl.multiple_of(u * 2 * ROWS, 16), 2 * ROWS)
-            high_ref[here] = high
-            low_ref[here] = low
-
+
+    def multiply(u):
+        values = []
+        for s in range(2):
+            lanes = pl.ds(pl.multiple_of((2 * u + s) * WIDE, 128), WIDE)
+            for a in range(PLANES // 2):
+                val = orb[16 * a : 16 * a + 16, lanes].astype(jnp.float32)
+                con = orb[48 + 16 * a : 64 + 16 * a, lanes].astype(jnp.float32)
+                first = pick(val[:8], slot_v) * pick(con[:8], slot_c)
+                second = pick(val[8:], slot_v) * pick(con[8:], slot_c)
+                values.append(jnp.where(upper, first, second))
+        high, low = halves(jnp.concatenate(values, 0))
+        here = pl.ds(pl.multiple_of(u * 2 * ROWS, 16), 2 * ROWS)
+        high_ref[here] = high
+        low_ref[here] = low
+
+    def transform(n):
         here = slice(n * group * ROWS, (n + 1) * group * ROWS)
         result = dot(high_ref[here], tz[...]) + dot(low_ref[here], tz[...])
         result = result[:, :128] + result[:, 128:]
         along_z[n * group : (n + 1) * group] = result.reshape(group, ROWS, 128)
+
+    for n in range(LOADS):
+        loads[n].wait()
+        if n > 0:
+            transform(n - 1)
+        for u in range(n * group // 2, (n + 1) * group // 2):
+            multiply(u)
+    transform(LOADS - 1)
 
     for copy in copies[6:]:
         copy.wait()
@@ -251,7 +263,7 @@
     sent = []
     for n, (e, d) in enumerate(OFFSETS):
         peer = ga_at(zl + turn * e, x + d)
-        block = ga_at(zl + turn * e + 2, x + d + 4 - y)
+        block = block_at(rem(zl + turn * e, 4), rem(x + d, 4))
         picked = dot(left[...], hot[block, :256])
         real = imag = jnp.zeros((8, BLOCK), jnp.float32)
         for a in range(ROWS // 8):
@@ -368,7 +380,7 @@
         for n, d in enumerate((2, 1, 3)):
             pass_col(step * 3 + n, d, col_slot(h, col_y, 0), col_y * 2 + h).wait_send()
         for n, d in enumerate((1, 3, 2)):
-            from_y = rem(col_y + d, 4)
+            from_y = mix(rem(x + d, 4), rem(i, 4))
             pass_col(0, d, col_slot(h, from_y, 0), from_y * 2 + h).wait_recv()
         blocks = -cols[pl.ds(h * 8, 8)]
         swapped = jnp.concatenate([-blocks[:, HERE:], blocks[:, :HERE]], 1)

time: 27.1 us -> 27.2 us (level)
  no operation moved by 1% of the time
where the time goes in v3:
time: 27.2 us; the launch traced here: 27 us
  Pallas kernels  26.2 us (96%)
  local copies, waits for them, and re-layouts  0.8 us (3%)
    pallas_call x1, Pallas kernels, coefficients(): pl.pallas_call(coefficients_kernel, out_shape=jax.ShapeDtypeStruct((2, BL...  26.2 us
    unnamed x1, local copies, waits for them, and re-layouts  0.8 us

profile of v3, /device:TPU:1, one launch (start us, length us, event | category | flops | bytes accessed | tf_op | source)
XLA Modules:
  0.0 27.0 jit_solution(14990539464355268416)
XLA Ops:
  0.0 26.2 %coefficients.1 = f32[2,256,256]{2,1,0:T(8,128)S(1)} custom-call(s32[2,8]{1,0:T(2,128)} %owner_in.1, s32[2,4]{1,0:T(2,128)} %bitcast.7, f32[8]{0:T(128)} %energy_v_in.1, f32[8]{0:T(128)} %energy_c_in.1, s32[1,4096]{1,0:T(1,128)} %bitcast.6, bf16[96,18432]{1,0:T(8,128)(2,1)} %bitcast.5, bf16[768,256]{1,0:T(8,128)(2,1)} %constant.6.clone.table_z, ...), custom_call_target="tpu_custom_call" | custom-call | tf_op jit(solution)/shard_map/coefficients/pallas_call | solution.py:398
  26.2 0.8 %copy.11 = f32[2,256,256]{2,1,0:T(8,128)} copy(f32[2,256,256]{2,1,0:T(8,128)S(1)} %coefficients.1) | data formatting | bytes 1048576

commit v4 on v2

--- a/solution.py
+++ b/solution.py
@@ -78,7 +78,7 @@
 
 def coefficients_kernel(
     owner_in, pairs_in, energy_v_in, energy_c_in, sphere_in, orbitals, table_z, table_y, table_x, out,
-    owner, pairs, energy_v, energy_c, sphere, orb, tz, ty, tx, high_ref, low_ref, along_z, hot, left, part, landed, total,
+    owner, pairs, energy_v, energy_c, sphere, orb, tz, ty, tx, split_ref, along_z, hot, left, part, landed, total,
     rows, cols, sems, send1, recv1, send_col, recv_col, send_row, recv_row, send_fc, recv_fc, send_fr, recv_fr,
 ):
     i, j = lax.axis_index("pair"), lax.axis_index("ga")
@@ -185,13 +185,12 @@
                     second = pick(val[8:], slot_v) * pick(con[8:], slot_c)
                     values.append(jnp.where(upper, first, second))
             high, low = halves(jnp.concatenate(values, 0))
-            here = pl.ds(pl.multiple_of(u * 2 * ROWS, 16), 2 * ROWS)
-            high_ref[here] = high
-            low_ref[here] = low
-
-        here = slice(n * group * ROWS, (n + 1) * group * ROWS)
-        result = dot(high_ref[here], tz[...]) + dot(low_ref[here], tz[...])
+            split_ref[n, pl.ds(pl.multiple_of((u - n * group // 2) * 2 * ROWS, 16), 2 * ROWS)] = high
+            split_ref[n, pl.ds(pl.multiple_of((u - n * group // 2) * 2 * ROWS + group * ROWS, 16), 2 * ROWS)] = low
+
+        result = dot(split_ref[n], tz[...])
         result = result[:, :128] + result[:, 128:]
+        result = result[: group * ROWS] + result[group * ROWS :]
         along_z[n * group : (n + 1) * group] = result.reshape(group, ROWS, 128)
 
     for copy in copies[6:]:
@@ -398,8 +397,7 @@
             pltpu.VMEM((WIDE, 256), jnp.bfloat16),
             pltpu.VMEM((2 * KY, 128), jnp.float32),
             pltpu.VMEM((4 * ROWS, 256), jnp.bfloat16),
-            pltpu.VMEM((CHUNKS * ROWS, WIDE), jnp.bfloat16),
-            pltpu.VMEM((CHUNKS * ROWS, WIDE), jnp.bfloat16),
+            pltpu.VMEM((LOADS, 2 * CHUNKS // LOADS * ROWS, WIDE), jnp.bfloat16),
             pltpu.VMEM((CHUNKS, ROWS, 128), jnp.float32),
             pltpu.VMEM((GROUPS, 256 + 16, BLOCK), jnp.bfloat16),
             pltpu.VMEM((8 * ROWS, 256), jnp.bfloat16),

time: 27.1 us -> 26.8 us (0.989)
  Pallas kernels: 26.2 us -> 25.9 us
    pallas_call x1, Pallas kernels: 26.2 us -> 25.9 us  [coefficients(): pl.pallas_call(coefficients_kernel, out_shape=jax.ShapeDtypeStruct((2, BL...]
where the time goes in v4:
time: 26.8 us; the launch traced here: 26.7 us
  Pallas kernels  25.9 us (97%)
  local copies, waits for them, and re-layouts  0.8 us (3%)
    pallas_call x1, Pallas kernels, coefficients(): pl.pallas_call(coefficients_kernel, out_shape=jax.ShapeDtypeStruct((2, BL...  25.9 us
    unnamed x1, local copies, waits for them, and re-layouts  0.8 us

profile of v4, /device:TPU:1, one launch (start us, length us, event | category | flops | bytes accessed | tf_op | source)
XLA Modules:
  0.0 26.7 jit_solution(6131718898728139570)
XLA Ops:
  0.0 25.9 %coefficients.1 = f32[2,256,256]{2,1,0:T(8,128)S(1)} custom-call(s32[2,8]{1,0:T(2,128)} %owner_in.1, s32[2,4]{1,0:T(2,128)} %bitcast.7, f32[8]{0:T(128)} %energy_v_in.1, f32[8]{0:T(128)} %energy_c_in.1, s32[1,4096]{1,0:T(1,128)} %bitcast.6, bf16[96,18432]{1,0:T(8,128)(2,1)} %bitcast.5, bf16[768,256]{1,0:T(8,128)(2,1)} %constant.6.clone.table_z, ...), custom_call_target="tpu_custom_call" | custom-call | tf_op jit(solution)/shard_map/coefficients/pallas_call | solution.py:385
  25.9 0.8 %copy.11 = f32[2,256,256]{2,1,0:T(8,128)} copy(f32[2,256,256]{2,1,0:T(8,128)S(1)} %coefficients.1) | data formatting | bytes 1048576

commit v5 on v4

--- a/solution.py
+++ b/solution.py
@@ -98,7 +98,7 @@
 
     moves = (
         (owner_in, owner), (pairs_in, pairs), (energy_v_in, energy_v), (energy_c_in, energy_c), (sphere_in, sphere),
-        (table_z, tz), (table_x.at[j], tx), (table_y, ty),
+        (table_z, tz.at[pl.ds(0, WIDE)]), (table_x.at[j], tx), (table_y, ty),
     )
     copies = [pltpu.make_async_copy(source, target, sems.at[LOADS + n]) for n, (source, target) in enumerate(moves)]
     loads = []
@@ -169,6 +169,7 @@
         return jnp.take_along_axis(value, slots, axis=0, mode="promise_in_bounds")
 
     copies[5].wait()
+    tz[WIDE:] = tz[:WIDE]
     group = CHUNKS // LOADS
     for n in range(LOADS):
         loads[n].wait()
@@ -185,12 +186,13 @@
                     second = pick(val[8:], slot_v) * pick(con[8:], slot_c)
                     values.append(jnp.where(upper, first, second))
             high, low = halves(jnp.concatenate(values, 0))
-            split_ref[n, pl.ds(pl.multiple_of((u - n * group // 2) * 2 * ROWS, 16), 2 * ROWS)] = high
-            split_ref[n, pl.ds(pl.multiple_of((u - n * group // 2) * 2 * ROWS + group * ROWS, 16), 2 * ROWS)] = low
-
-        result = dot(split_ref[n], tz[...])
+            here = pl.ds(pl.multiple_of(u * 2 * ROWS, 16), 2 * ROWS)
+            split_ref[here, :WIDE] = high
+            split_ref[here, WIDE:] = low
+
+        here = slice(n * group * ROWS, (n + 1) * group * ROWS)
+        result = dot(split_ref[here], tz[...])
         result = result[:, :128] + result[:, 128:]
-        result = result[: group * ROWS] + result[group * ROWS :]
         along_z[n * group : (n + 1) * group] = result.reshape(group, ROWS, 128)
 
     for copy in copies[6:]:
@@ -394,10 +396,10 @@
             pltpu.SMEM((8,), jnp.float32),
             pltpu.VMEM((1, NG), jnp.int32),
             pltpu.VMEM((16 * PLANES, points), jnp.bfloat16),
-            pltpu.VMEM((WIDE, 256), jnp.bfloat16),
+            pltpu.VMEM((2 * WIDE, 256), jnp.bfloat16),
             pltpu.VMEM((2 * KY, 128), jnp.float32),
             pltpu.VMEM((4 * ROWS, 256), jnp.bfloat16),
-            pltpu.VMEM((LOADS, 2 * CHUNKS // LOADS * ROWS, WIDE), jnp.bfloat16),
+            pltpu.VMEM((CHUNKS * ROWS, 2 * WIDE), jnp.bfloat16),
             pltpu.VMEM((CHUNKS, ROWS, 128), jnp.float32),
             pltpu.VMEM((GROUPS, 256 + 16, BLOCK), jnp.bfloat16),
             pltpu.VMEM((8 * ROWS, 256), jnp.bfloat16),

time: 26.8 us -> 26.9 us (level)
  no operation moved by 1% of the time
where the time goes in v5:
time: 26.9 us; the launch traced here: 26.8 us
  Pallas kernels  25.9 us (96%)
  local copies, waits for them, and re-layouts  0.8 us (3%)
    pallas_call x1, Pallas kernels, coefficients(): pl.pallas_call(coefficients_kernel, out_shape=jax.ShapeDtypeStruct((2, BL...  25.9 us
    unnamed x1, local copies, waits for them, and re-layouts  0.8 us

profile of v5, /device:TPU:1, one launch (start us, length us, event | category | flops | bytes accessed | tf_op | source)
XLA Modules:
  0.0 26.8 jit_solution(257307278589284379)
XLA Ops:
  0.0 25.9 %coefficients.1 = f32[2,256,256]{2,1,0:T(8,128)S(1)} custom-call(s32[2,8]{1,0:T(2,128)} %owner_in.1, s32[2,4]{1,0:T(2,128)} %bitcast.7, f32[8]{0:T(128)} %energy_v_in.1, f32[8]{0:T(128)} %energy_c_in.1, s32[1,4096]{1,0:T(1,128)} %bitcast.6, bf16[96,18432]{1,0:T(8,128)(2,1)} %bitcast.5, bf16[768,256]{1,0:T(8,128)(2,1)} %constant.6.clone.table_z, ...), custom_call_target="tpu_custom_call" | custom-call | tf_op jit(solution)/shard_map/coefficients/pallas_call | solution.py:387
  26.0 0.8 %copy.11 = f32[2,256,256]{2,1,0:T(8,128)} copy(f32[2,256,256]{2,1,0:T(8,128)S(1)} %coefficients.1) | data formatting | bytes 1048576
